TPU v7x, 32 devices: a whole 2x2x4 slice. The times are simulated.
32 devices in a mesh: dp: 4 (over y, core), factor: 8 (over z, x).
Axes of the slice: x: 2, y: 2, z: 4, core: 2. Of those that a mesh axis runs over, the one named last changes fastest.
Arguments:
- activations: bfloat16 [512, 8192], P('dp', 'factor'), may hold values from -12 to 12
- gradients: bfloat16 [512, 8192], P('dp', 'factor'), may hold values from -12 to 12
- act_basis: bfloat16 [8192, 8192], P('dp', 'factor'), may hold values from -0.0625 to 0.0625
- grad_basis: bfloat16 [8192, 8192], P('dp', 'factor'), may hold values from -0.0625 to 0.0625
Outputs:
- corrected: float32 [8192, 8192], P('factor', 'dp')
All inputs are finite; a program needn't handle non-finite values.
Results may differ from a plain program's by a relative error of at most 0.00062.
Values may be sent and summed in bfloat16 or wider, within the bound.
A program may use at most 128 MiB of HBM per device.

v0:
```python
import jax
import jax.numpy as jnp
from jax import lax
from jax.sharding import PartitionSpec as P


def on_device(activations, gradients, act_basis, grad_basis):
    act_full, grad_full = (
        lax.all_gather(activations, "factor", axis=1, tiled=True),
        lax.all_gather(gradients, "factor", axis=1, tiled=True),
    )
    columns = act_full
    rotated_act = jnp.dot(
        columns,
        lax.all_gather(act_basis, "dp", axis=0, tiled=True),
        preferred_element_type=jnp.float32,
    )
    columns = grad_full
    rotated_grad = jnp.dot(
        columns,
        lax.all_gather(grad_basis, "dp", axis=0, tiled=True),
        preferred_element_type=jnp.float32,
    )
    act_square = (rotated_act * rotated_act).astype(jnp.bfloat16)
    grad_square = (rotated_grad * rotated_grad).astype(jnp.bfloat16)
    act_every = lax.all_gather(act_square, "dp", axis=0, tiled=True)
    grad_wide = lax.all_gather(grad_square, "factor", axis=1, tiled=True)
    grad_block = lax.all_to_all(grad_wide, "dp", split_axis=1, concat_axis=0, tiled=True)
    total = lax.dot_general(
        act_every, grad_block, (((0,), (0,)), ((), ())), preferred_element_type=jnp.float32
    )
    return total * (1.0 / act_every.shape[0])


def solution(mesh):
    return jax.shard_map(
        on_device,
        mesh=mesh,
        in_specs=(P("dp", "factor"), P("dp", "factor"), P("dp", "factor"), P("dp", "factor")),
        out_specs=P("factor", "dp"),
        check_vma=False,
    )
```

profile of v0, /device:TPU:29, one launch (start us, length us, event | category | flops | bytes accessed | tf_op | source)
XLA Modules:
  0.0 423.8 jit_solution(3426008681115056997)
XLA Ops:
  6.5 0.0 all-gather.13.cloned.1.call-start
  6.5 0.7 all-gather.13.cloned.1.call-update
  7.3 0.0 all-gather.15.cloned.1.call-start
  7.3 0.7 all-gather.15.cloned.1.call-update
  8.0 0.0 all-gather.7.cloned.1.call-start
  8.1 0.7 all-gather.7.cloned.1.call-update
  8.7 0.0 all-gather.9.cloned.1.call-start
  8.8 0.5 all-gather.9.cloned.1.call-update
  9.3 0.0 all-gather.17.cloned.1.call-start
  9.4 48.8 %all-gather.13.cloned.1.call-done = bf16[128,8192]{1,0:T(8,128)(2,1)} async-done(((bf16[128,1024]{1,0:T(8,128)(2,1)}), bf16[128,8192]{1,0:T(8,128)(2,1)}) %all-gather.13.cloned.1.call-update) | async-done | bytes 2097168 | tf_op jit(solution)/shard_map/all_gather | solution.py:10
  58.2 107.1 %all-gather.15.cloned.1.call-done = bf16[8192,1024]{1,0:T(8,128)(2,1)} async-done(((bf16[2048,1024]{1,0:T(8,128)(2,1)}), bf16[8192,1024]{1,0:T(8,128)(2,1)}) %all-gather.15.cloned.1.call-update) | async-done | bytes 16777232 | tf_op jit(solution)/shard_map/all_gather | solution.py:21
  165.3 9.4 %fusion.1 = bf16[128,1024]{1,0:T(8,128)(2,1)} fusion(bf16[128,8192]{1,0:T(8,128)(2,1)} %all-gather.13.cloned.1.call-done, bf16[8192,1024]{1,0:T(8,128)(2,1)} %all-gather.15.cloned.1.call-done), kind=kOutput, calls=%fused_computation.5 | convolution fusion | flops 2147745792 | bytes 19136512 | tf_op jit(solution)/shard_map/dot_general | solution.py:19
  174.7 0.0 all-gather.17.cloned.1.call-update
  174.8 0.0 all-gather.11.cloned.1.call-start
  174.8 40.9 %all-gather.7.cloned.1.call-done = bf16[128,8192]{1,0:T(8,128)(2,1)} async-done(((bf16[128,1024]{1,0:T(8,128)(2,1)}), bf16[128,8192]{1,0:T(8,128)(2,1)}) %all-gather.7.cloned.1.call-update) | async-done | bytes 2097168 | tf_op jit(solution)/shard_map/all_gather | solution.py:9
  215.7 106.9 %all-gather.9.cloned.1.call-done = bf16[8192,1024]{1,0:T(8,128)(2,1)} async-done(((bf16[2048,1024]{1,0:T(8,128)(2,1)}), bf16[8192,1024]{1,0:T(8,128)(2,1)}) %all-gather.9.cloned.1.call-update) | async-done | bytes 16777232 | tf_op jit(solution)/shard_map/all_gather | solution.py:15
  322.6 9.4 %fusion = bf16[128,1024]{1,0:T(8,128)(2,1)} fusion(bf16[128,8192]{1,0:T(8,128)(2,1)} %all-gather.7.cloned.1.call-done, bf16[8192,1024]{1,0:T(8,128)(2,1)} %all-gather.9.cloned.1.call-done), kind=kOutput, calls=%fused_computation.4 | convolution fusion | flops 2147745792 | bytes 19136512 | tf_op jit(solution)/shard_map/dot_general | solution.py:13
  332.1 0.0 all-gather.11.cloned.1.call-update
  332.1 40.8 %all-gather.17.cloned.1.call-done = bf16[128,8192]{1,0:T(8,128)(2,1)} async-done(((bf16[128,1024]{1,0:T(8,128)(2,1)}), bf16[128,8192]{1,0:T(8,128)(2,1)}) %all-gather.17.cloned.1.call-update) | async-done | bytes 2097168 | tf_op jit(solution)/shard_map/all_gather | solution.py:27
  372.9 3.2 copy.8
  376.1 4.5 %all-to-all-start = ((bf16[128,4,2048]{2,0,1:T(8,128)(2,1)}), bf16[128,4,2048]{2,0,1:T(8,128)(2,1)S(1)}, u32[]{:S(2)}, u32[]{:S(2)}) async-start(bf16[128,4,2048]{2,0,1:T(8,128)(2,1)} %bitcast.12), calls=%async_computation | async-start | bytes 4194304 | tf_op jit(solution)/shard_map/all_to_all | solution.py:28
  380.6 15.7 %all-gather.11.cloned.1.call-done = bf16[512,1024]{1,0:T(8,128)(2,1)} async-done(((bf16[128,1024]{1,0:T(8,128)(2,1)}), bf16[512,1024]{1,0:T(8,128)(2,1)}) %all-gather.11.cloned.1.call-update) | async-done | bytes 1048592 | tf_op jit(solution)/shard_map/all_gather | solution.py:26
  396.3 13.7 %all-to-all-done = bf16[128,4,2048]{2,0,1:T(8,128)(2,1)S(1)} async-done(((bf16[128,4,2048]{2,0,1:T(8,128)(2,1)}), bf16[128,4,2048]{2,0,1:T(8,128)(2,1)S(1)}, u32[]{:S(2)}, u32[]{:S(2)}) %all-to-all-start) | async-done | bytes 2097184 | tf_op jit(solution)/shard_map/all_to_all | solution.py:28
  410.0 7.0 %convolution_multiply_fusion = f32[1024,2048]{1,0:T(8,128)} fusion(bf16[512,1024]{1,0:T(8,128)(2,1)} %all-gather.11.cloned.1.call-done, bf16[512,2048]{1,0:T(8,128)(2,1)S(1)} %bitcast.14), kind=kOutput, calls=%fused_computation | convolution fusion | flops 2149580800 | bytes 11534336 | tf_op jit(solution)/shard_map/dot_general | solution.py:29
Async XLA Ops:
  6.5 51.7 %all-gather.13.cloned.1.call-start = ((), (), s32[]{:S(2)}) async-start(), calls=%async_computation.4 | async-start | bytes 2359296 | tf_op jit(solution)/shard_map/all_gather | solution.py:10
  7.3 158.0 %all-gather.15.cloned.1.call-start = ((), (), s32[]{:S(2)}) async-start(), calls=%async_computation.5 | async-start | bytes 20971520 | tf_op jit(solution)/shard_map/all_gather | solution.py:21
  8.0 207.7 %all-gather.7.cloned.1.call-start = ((), (), s32[]{:S(2)}) async-start(), calls=%async_computation.1 | async-start | bytes 2359296 | tf_op jit(solution)/shard_map/all_gather | solution.py:9
  8.7 313.9 %all-gather.9.cloned.1.call-start = ((), (), s32[]{:S(2)}) async-start(), calls=%async_computation.2 | async-start | bytes 20971520 | tf_op jit(solution)/shard_map/all_gather | solution.py:15
  9.3 363.6 %all-gather.17.cloned.1.call-start = ((), (), s32[]{:S(2)}) async-start(), calls=%async_computation.6 | async-start | bytes 2359296 | tf_op jit(solution)/shard_map/all_gather | solution.py:27
  174.8 221.5 %all-gather.11.cloned.1.call-start = ((), (), s32[]{:S(2)}) async-start(), calls=%async_computation.3 | async-start | bytes 1310720 | tf_op jit(solution)/shard_map/all_gather | solution.py:26
  376.1 33.9 %all-to-all-start = ((bf16[128,4,2048]{2,0,1:T(8,128)(2,1)}), bf16[128,4,2048]{2,0,1:T(8,128)(2,1)S(1)}, u32[]{:S(2)}, u32[]{:S(2)}) async-start(bf16[128,4,2048]{2,0,1:T(8,128)(2,1)} %bitcast.12), calls=%async_computation | async-start | bytes 4194304 | tf_op jit(solution)/shard_map/all_to_all | solution.py:28
Sparse Core Ops, SparseCore 0:
  9.5 48.6 all-gather.12
  59.8 105.4 all-gather.14
  167.5 48.1 all-gather.6
  217.1 105.4 all-gather.8
  324.7 48.1 all-gather.16
  374.3 21.8 all-gather.10
where the time goes:
time: 428 us; the launch traced here: 424 us
  waiting for transfers between devices  377 us (88%)
  matrix products  25.9 us (6%)
  between operations  13.5 us (3%)
  starting transfers between devices  4.7 us (1%)
    all_gather x1, waiting for transfers between devices, on_device(): lax.all_gather(grad_basis, 'dp', axis=0, tiled=True)  107 us
    all_gather x1, waiting for transfers between devices, on_device(): lax.all_gather(act_basis, 'dp', axis=0, tiled=True)  107 us
    all_gather x1, waiting for transfers between devices, on_device(): lax.all_gather(gradients, 'factor', axis=1, tiled=True)  48.8 us
    all_gather x1, waiting for transfers between devices, on_device(): lax.all_gather(activations, 'factor', axis=1, tiled=True)  40.9 us
    all_gather x1, waiting for transfers between devices, on_device(): grad_wide = lax.all_gather(grad_square, 'factor', axis=1, tiled=True)  40.8 us
    all_gather x1, waiting for transfers between devices, on_device(): act_every = lax.all_gather(act_square, 'dp', axis=0, tiled=True)  15.7 us
    all_to_all x1, waiting for transfers between devices, on_device(): lax.all_to_all(grad_wide, 'dp', split_axis=1, concat_axis=0, tiled=True)  13.7 us
    dot_general x1, matrix products, on_device(): jnp.dot(columns, lax.all_gather(grad_basis, 'dp', axis=0, tiled=True), pr...  9.45 us
  transfers between devices with their start and end apart: 7, of which 7 were waited for; matrix products, arithmetic and copies ran while one was open for 5% of the time, Pallas kernels for 0%

commit v1 on v0

v1 whole, which is shorter than its diff:
```python
import jax
import jax.numpy as jnp
from jax import lax
from jax.sharding import PartitionSpec as P


def rows_of_block(block):
    wide = lax.all_gather(block, "factor", axis=1, tiled=True)
    return lax.all_to_all(wide, "dp", split_axis=1, concat_axis=0, tiled=True)


def squared(block, basis):
    part = jnp.dot(rows_of_block(block), basis, preferred_element_type=jnp.float32)
    rotated = lax.psum_scatter(part, "dp", scatter_dimension=0, tiled=True)
    return (rotated * rotated).astype(jnp.bfloat16)


def on_device(activations, gradients, act_basis, grad_basis):
    grad_square = squared(gradients, grad_basis)
    act_square = squared(activations, act_basis)
    act_every = lax.all_gather(act_square, "dp", axis=0, tiled=True)
    grad_block = rows_of_block(grad_square)
    total = lax.dot_general(
        act_every, grad_block, (((0,), (0,)), ((), ())), preferred_element_type=jnp.float32
    )
    return total * (1.0 / act_every.shape[0])


def solution(mesh):
    return jax.shard_map(
        on_device,
        mesh=mesh,
        in_specs=(P("dp", "factor"), P("dp", "factor"), P("dp", "factor"), P("dp", "factor")),
        out_specs=P("factor", "dp"),
        check_vma=False,
    )
```

time: 428 us -> 292 us (0.68)
  waiting for transfers between devices: 377 us -> 170 us
  blocking collectives: 0 us -> 63.7 us
  local copies, waits for them, and re-layouts: 3.16 us -> 11.9 us
  matrix products: 25.9 us -> 20 us
    all_gather x5 -> x3, waiting for transfers between devices: 345 us -> 109 us  [rows_of_block(): wide = lax.all_gather(block, 'factor', axis=1, tiled=True)]
    all_to_all x0 -> x2, blocking collectives: none -> 63.7 us  [rows_of_block(): return lax.all_to_all(wide, 'dp', split_axis=1, concat_axis=0, tiled=True)]
    reduce_scatter x0 -> x2, waiting for transfers between devices: none -> 30.9 us  [squared(): rotated = lax.psum_scatter(part, 'dp', scatter_dimension=0, tiled=True)]
    dot_general x2, matrix products: 18.9 us -> 13 us  [squared(): jnp.dot(rows_of_block(block), basis, preferred_element_type=jnp.float32)]
    all_to_all x1 -> x3, local copies, waits for them, and re-layouts: 3.16 us -> 8.32 us  [rows_of_block(): return lax.all_to_all(wide, 'dp', split_axis=1, concat_axis=0, tiled=True)]
  transfers between devices with their start and end apart: 7 -> 7, of which waited for: 7 -> 6; matrix products, arithmetic and copies ran while one was open for 5% -> 9% of each run, Pallas kernels for 0% -> 0%
where the time goes in v1:
time: 292 us; the launch traced here: 287 us
  waiting for transfers between devices  170 us (58%)
  blocking collectives  63.7 us (22%)
  matrix products  20 us (7%)
  between operations  13.5 us (5%)
  local copies, waits for them, and re-layouts  11.9 us (4%)
  starting transfers between devices  4.72 us (2%)
  other arithmetic  3.56 us (1%)
    all_gather x3, waiting for transfers between devices, rows_of_block(): wide = lax.all_gather(block, 'factor', axis=1, tiled=True)  109 us
    all_to_all x2, blocking collectives, rows_of_block(): return lax.all_to_all(wide, 'dp', split_axis=1, concat_axis=0, tiled=True)  63.7 us
    reduce_scatter x2, waiting for transfers between devices, squared(): rotated = lax.psum_scatter(part, 'dp', scatter_dimension=0, tiled=True)  30.9 us
    all_gather x1, waiting for transfers between devices, on_device(): act_every = lax.all_gather(act_square, 'dp', axis=0, tiled=True)  15.7 us
    all_to_all x1, waiting for transfers between devices, rows_of_block(): return lax.all_to_all(wide, 'dp', split_axis=1, concat_axis=0, tiled=True)  13.7 us
    dot_general x2, matrix products, squared(): jnp.dot(rows_of_block(block), basis, preferred_element_type=jnp.float32)  13 us
    all_to_all x3, local copies, waits for them, and re-layouts, rows_of_block(): return lax.all_to_all(wide, 'dp', split_axis=1, concat_axis=0, tiled=True)  8.32 us
    dot_general x1, matrix products, on_device(): lax.dot_general(act_every, grad_block, (((0,), (0,)), ((), ())), preferre...  7.01 us
  transfers between devices with their start and end apart: 7, of which 6 were waited for; matrix products, arithmetic and copies ran while one was open for 9% of the time, Pallas kernels for 0%

profile of v1, /device:TPU:29, one launch (start us, length us, event | category | flops | bytes accessed | tf_op | source)
XLA Modules:
  0.0 287.0 jit_solution(12247298543048865413)
XLA Ops:
  6.5 0.0 all-gather.9.cloned.1.call-start
  6.5 1.8 copy.8
  8.3 0.0 all-gather.9.cloned.1.call-update
  8.4 0.0 all-gather.5.cloned.1.call-start
  8.4 1.8 copy.6
  10.2 0.0 all-gather.5.cloned.1.call-update
  10.2 0.0 reduce-scatter.5.cloned.1.call-start
  10.3 47.9 %all-gather.9.cloned.1.call-done = bf16[128,8192]{0,1:T(8,128)(2,1)} async-done(((bf16[128,1024]{0,1:T(8,128)(2,1)}), bf16[128,8192]{0,1:T(8,128)(2,1)}) %all-gather.9.cloned.1.call-update) | async-done | bytes 2097168 | tf_op jit(solution)/shard_map/all_gather | solution.py:8
  58.2 28.3 %all_to_all.57 = bf16[128,4,2048]{0,2,1:T(8,128)(2,1)S(1)} all-to-all(bf16[128,4,2048]{0,2,1:T(8,128)(2,1)} %bitcast.23), channel_id=1, replica_groups=mesh['dp'=4,'factor'=8] {'dp'}, dimensions={1} | all-to-all | bytes 4194304 | tf_op jit(solution)/shard_map/all_to_all | solution.py:9
  86.4 2.6 copy.9
  89.0 6.5 %fusion.1 = f32[512,1024]{1,0:T(8,128)} fusion(bf16[512,2048]{1,0:T(8,128)(2,1)} %bitcast.25, bf16[2048,1024]{1,0:T(8,128)(2,1)} %param.7), kind=kOutput, calls=%fused_computation.5 | convolution fusion | flops 2147483648 | bytes 8388608 | tf_op jit(solution)/shard_map/dot_general | solution.py:13
  95.5 0.0 reduce-scatter.5.cloned.1.call-update
  95.6 0.0 reduce-scatter.3.cloned.1.call-start
  95.6 12.5 %all-gather.5.cloned.1.call-done = bf16[128,8192]{0,1:T(8,128)(2,1)} async-done(((bf16[128,1024]{0,1:T(8,128)(2,1)}), bf16[128,8192]{0,1:T(8,128)(2,1)}) %all-gather.5.cloned.1.call-update) | async-done | bytes 2097168 | tf_op jit(solution)/shard_map/all_gather | solution.py:8
  108.1 35.4 %all_to_all.58 = bf16[128,4,2048]{0,2,1:T(8,128)(2,1)S(1)} all-to-all(bf16[128,4,2048]{0,2,1:T(8,128)(2,1)} %bitcast.21), channel_id=1, replica_groups=mesh['dp'=4,'factor'=8] {'dp'}, dimensions={1} | all-to-all | bytes 4194304 | tf_op jit(solution)/shard_map/all_to_all | solution.py:9
  143.5 2.6 copy.7
  146.1 6.5 %fusion = f32[512,1024]{1,0:T(8,128)} fusion(bf16[512,2048]{1,0:T(8,128)(2,1)} %bitcast.26, bf16[2048,1024]{1,0:T(8,128)(2,1)} %param.6), kind=kOutput, calls=%fused_computation.4 | convolution fusion | flops 2147483648 | bytes 8388608 | tf_op jit(solution)/shard_map/dot_general | solution.py:13
  152.6 0.0 reduce-scatter.3.cloned.1.call-update
  152.6 0.0 all-gather.11.cloned.1.call-start
  152.7 0.0 reduce-scatter.5.cloned.1.call-done
  152.7 1.8 multiply_convert_fusion
  154.5 0.0 all-gather.11.cloned.1.call-update
  154.5 0.0 all-gather.7.cloned.1.call-start
  154.5 30.9 %reduce-scatter.3.cloned.1.call-done = f32[128,1024]{1,0:T(8,128)} async-done(((f32[512,1024]{1,0:T(8,128)}), f32[128,1024]{1,0:T(8,128)}) %reduce-scatter.3.cloned.1.call-update) | async-done | bytes 524304 | tf_op jit(solution)/shard_map/reduce_scatter | solution.py:14
  185.4 1.8 multiply_convert_fusion.1
  187.2 0.0 all-gather.7.cloned.1.call-update
  187.2 48.9 %all-gather.11.cloned.1.call-done = bf16[128,8192]{1,0:T(8,128)(2,1)} async-done(((bf16[128,1024]{1,0:T(8,128)(2,1)}), bf16[128,8192]{1,0:T(8,128)(2,1)}) %all-gather.11.cloned.1.call-update) | async-done | bytes 2097168 | tf_op jit(solution)/shard_map/all_gather | solution.py:8
  236.1 3.2 %copy.13 = bf16[16,4,8,2048]{3,2,0,1:T(8,128)(2,1)} copy(bf16[16,4,8,2048]{3,2,1,0:T(8,128)(2,1)} %bitcast.22) | data formatting | bytes 4194304 | tf_op jit(solution)/shard_map/all_to_all | solution.py:9
  239.2 4.5 %all-to-all-start.2 = ((bf16[128,4,2048]{2,0,1:T(8,128)(2,1)}), bf16[128,4,2048]{2,0,1:T(8,128)(2,1)S(1)}, u32[]{:S(2)}, u32[]{:S(2)}) async-start(bf16[128,4,2048]{2,0,1:T(8,128)(2,1)} %bitcast.18), calls=%async_computation.4 | async-start | bytes 4194304 | tf_op jit(solution)/shard_map/all_to_all | solution.py:9
  243.7 15.7 %all-gather.7.cloned.1.call-done = bf16[512,1024]{1,0:T(8,128)(2,1)} async-done(((bf16[128,1024]{1,0:T(8,128)(2,1)}), bf16[512,1024]{1,0:T(8,128)(2,1)}) %all-gather.7.cloned.1.call-update) | async-done | bytes 1048592 | tf_op jit(solution)/shard_map/all_gather | solution.py:21
  259.4 13.7 %all-to-all-done.2 = bf16[128,4,2048]{2,0,1:T(8,128)(2,1)S(1)} async-done(((bf16[128,4,2048]{2,0,1:T(8,128)(2,1)}), bf16[128,4,2048]{2,0,1:T(8,128)(2,1)S(1)}, u32[]{:S(2)}, u32[]{:S(2)}) %all-to-all-start.2) | async-done | bytes 2097184 | tf_op jit(solution)/shard_map/all_to_all | solution.py:9
  273.2 7.0 %convolution_multiply_fusion = f32[1024,2048]{1,0:T(8,128)} fusion(bf16[512,1024]{1,0:T(8,128)(2,1)} %all-gather.7.cloned.1.call-done, bf16[512,2048]{1,0:T(8,128)(2,1)S(1)} %bitcast.24), kind=kOutput, calls=%fused_computation | convolution fusion | flops 2149580800 | bytes 11534336 | tf_op jit(solution)/shard_map/dot_general | solution.py:23
Async XLA Ops:
  6.5 51.6 %all-gather.9.cloned.1.call-start = ((), (), s32[]{:S(2)}) async-start(), calls=%async_computation.8 | async-start | bytes 2359296 | tf_op jit(solution)/shard_map/all_gather | solution.py:8
  8.4 99.7 %all-gather.5.cloned.1.call-start = ((), (), s32[]{:S(2)}) async-start(), calls=%async_computation.5 | async-start | bytes 2359296 | tf_op jit(solution)/shard_map/all_gather | solution.py:8
  10.2 142.5 %reduce-scatter.5.cloned.1.call-start = ((), (), s32[]{:S(2)}) async-start(), calls=%async_computation.9 | async-start | bytes 2621440 | tf_op jit(solution)/shard_map/reduce_scatter | solution.py:14
  95.6 89.8 %reduce-scatter.3.cloned.1.call-start = ((), (), s32[]{:S(2)}) async-start(), calls=%async_computation.6 | async-start | bytes 2621440 | tf_op jit(solution)/shard_map/reduce_scatter | solution.py:14
  152.6 83.5 %all-gather.11.cloned.1.call-start = ((), (), s32[]{:S(2)}) async-start(), calls=%async_computation.10 | async-start | bytes 2359296 | tf_op jit(solution)/shard_map/all_gather | solution.py:8
  154.5 104.9 %all-gather.7.cloned.1.call-start = ((), (), s32[]{:S(2)}) async-start(), calls=%async_computation.7 | async-start | bytes 1310720 | tf_op jit(solution)/shard_map/all_gather | solution.py:21
  239.2 33.9 %all-to-all-start.2 = ((bf16[128,4,2048]{2,0,1:T(8,128)(2,1)}), bf16[128,4,2048]{2,0,1:T(8,128)(2,1)S(1)}, u32[]{:S(2)}, u32[]{:S(2)}) async-start(bf16[128,4,2048]{2,0,1:T(8,128)(2,1)} %bitcast.18), calls=%async_computation.4 | async-start | bytes 4194304 | tf_op jit(solution)/shard_map/all_to_all | solution.py:9
Sparse Core Ops, SparseCore 0:
  9.5 48.6 all-gather.8
  60.3 47.7 all-gather.4
  110.6 38.2 reduce-scatter.4
  152.7 32.6 reduce-scatter.2
  187.4 48.5 all-gather.10
  237.5 21.8 all-gather.6

commit v2 on v1

v2 whole, which is shorter than its diff:
```python
import functools

import jax
import jax.numpy as jnp
from jax import lax
from jax.experimental import pallas as pl
from jax.experimental.pallas import tpu as pltpu
from jax.sharding import PartitionSpec as P

MESH = pl.DeviceIdType.MESH
TILE = 256


def kernel(
    nd, na,
    grad_hbm, act_hbm, grad_basis_hbm, act_basis_hbm,
    act_out, grad_out,
    basis, line, held, part, pair, tail, sq_line, sq_held, every,
    load_sem, z_send, z_recv, y_send, y_recv, x_send, x_recv,
    pair_send, pair_recv, tail_send, tail_recv, sq_send, sq_recv, fan_send, fan_recv,
):
    d, f = lax.axis_index("dp"), lax.axis_index("factor")
    o, c = d // 2, lax.rem(d, 2)
    a, b = f // 2, lax.rem(f, 2)
    no = nd // 2

    def along_line(i):
        return lax.rem(a + i, na)

    def along_dp(i):
        return lax.rem(d + i, nd)

    def along_outer(i):
        return lax.rem(o + i, no)

    def remote(src, dst, send, recv, device):
        return pltpu.make_async_remote_copy(
            src_ref=src, dst_ref=dst, send_sem=send, recv_sem=recv,
            device_id=device, device_id_type=MESH,
        )

    across = (d, a * 2 + 1 - b)
    partner = (o * 2 + 1 - c, f)

    loads = [
        pltpu.make_async_copy(grad_hbm, line.at[0, a], load_sem.at[0]),
        pltpu.make_async_copy(act_hbm, line.at[1, a], load_sem.at[1]),
        pltpu.make_async_copy(grad_basis_hbm, basis.at[0], load_sem.at[2]),
        pltpu.make_async_copy(act_basis_hbm, basis.at[1], load_sem.at[3]),
    ]
    for load in loads:
        load.start()

    barrier = pltpu.get_barrier_semaphore()
    for i in range(1, na):
        pl.semaphore_signal(barrier, inc=1, device_id=(d, along_line(i) * 2 + b), device_id_type=MESH)
    for i in range(1, nd):
        pl.semaphore_signal(barrier, inc=1, device_id=(along_dp(i), f), device_id_type=MESH)
    pl.semaphore_signal(barrier, inc=1, device_id=across, device_id_type=MESH)
    pl.semaphore_wait(barrier, na + nd - 1)

    class Redistribute:
        def __init__(self, m, lines, blocks):
            self.m, self.lines, self.blocks = m, lines, blocks

        def line_copy(self, i, slot):
            m = self.m
            return remote(
                self.lines.at[a], self.lines.at[slot], z_send.at[m, i], z_recv.at[m, slot],
                (d, along_line(i) * 2 + b),
            )

        def dp_copy(self, panel, slot):
            m = self.m
            return remote(
                self.lines.at[panel], self.blocks.at[b, slot], y_send.at[m, panel], y_recv.at[m, slot],
                (panel, f),
            )

        def side_copy(self, side, rows):
            m = self.m
            return remote(
                self.blocks.at[side, rows], self.blocks.at[side, rows],
                x_send.at[m, rows], x_recv.at[m, rows], across,
            )

        def start_line(self):
            for i in range(1, na):
                self.line_copy(i, a).start()

        def forward_dp(self, steps):
            for i in steps:
                panel = along_line(i)
                if i:
                    self.line_copy(i, panel).wait_recv()

                @pl.when(panel != d)
                def _():
                    self.dp_copy(panel, d).start()

                @pl.when(panel == d)
                def _():
                    self.blocks[b, d] = self.lines[panel]
                    self.side_copy(b, d).start()

        def forward_side(self, steps):
            for i in steps:
                rows = along_dp(i)
                self.dp_copy(d, rows).wait_recv()
                self.side_copy(b, rows).start()

        def wait_side(self):
            for i in range(nd):
                self.side_copy(1 - b, along_dp(i)).wait_recv()

        def wait_sends(self):
            for i in range(1, na):
                self.line_copy(i, a).wait_send()
            for i in range(na):
                panel = along_line(i)

                @pl.when(panel != d)
                def _():
                    self.dp_copy(panel, d).wait_send()
            for i in range(nd):
                self.side_copy(b, along_dp(i)).wait_send()

    width = part.shape[-1]
    rows = held.shape[2] * held.shape[3]

    def multiply(m):
        @pl.loop(0, width // TILE)
        def _(tile):
            columns = pl.ds(pl.multiple_of(tile * TILE, TILE), TILE)
            depth = held.shape[4]
            total = jnp.dot(
                held[m, 0].reshape(rows, depth), basis[m, pl.ds(0, depth), columns],
                preferred_element_type=jnp.float32,
            ) + jnp.dot(
                held[m, 1].reshape(rows, depth), basis[m, pl.ds(depth, depth), columns],
                preferred_element_type=jnp.float32,
            )
            part[m, :, :, columns] = total.reshape(nd, rows // nd, TILE)

    def pair_copy(m, outer, core):
        return remote(
            part.at[m, outer * 2 + core], pair.at[m, outer],
            pair_send.at[m, outer], pair_recv.at[m, outer], partner,
        )

    def tail_copy(m, outer, slot):
        return remote(
            part.at[m, outer * 2 + c], tail.at[m, slot],
            tail_send.at[m, outer], tail_recv.at[m, slot], (outer * 2 + c, f),
        )

    def start_pair(m):
        for i in range(1, no + 1):
            pair_copy(m, along_outer(i), 1 - c).start()

    def start_tail(m):
        for i in range(1, no + 1):
            outer = along_outer(i)
            pair_copy(m, outer, c).wait_recv()
            part[m, outer * 2 + c] += pair[m, outer]
            if i < no:
                tail_copy(m, outer, o).start()

    def squared(m):
        total = part[m, d]
        for i in range(1, no):
            outer = along_outer(i)
            tail_copy(m, outer, outer).wait_recv()
            total = total + tail[m, outer]
        return (total * total).astype(jnp.bfloat16)

    def wait_sums(m):
        for i in range(1, no + 1):
            pair_copy(m, along_outer(i), 1 - c).wait_send()
            if i < no:
                tail_copy(m, along_outer(i), o).wait_send()

    grad = Redistribute(0, line.at[0], held.at[0])
    act = Redistribute(1, line.at[1], held.at[1])
    square = Redistribute(2, sq_line, sq_held)

    loads[0].wait()
    grad.start_line()
    loads[1].wait()
    act.start_line()
    grad.forward_dp(range(na))
    act.forward_dp(range(1))
    grad.forward_side(range(1, nd))
    act.forward_dp(range(1, na - 1))
    loads[2].wait()
    grad.wait_side()
    multiply(0)
    start_pair(0)
    act.forward_dp(range(na - 1, na))
    start_tail(0)
    act.forward_side(range(1, nd))
    loads[3].wait()

    sq_line[a] = squared(0)
    square.start_line()
    square.forward_dp(range(1))
    act.wait_side()
    multiply(1)
    start_pair(1)
    start_tail(1)
    square.forward_dp(range(1, na))
    square.forward_side(range(1, nd))

    every[d] = squared(1)

    def cross_copy(outer, slot):
        return remote(
            every.at[d], every.at[slot], sq_send.at[outer], sq_recv.at[slot // 2], (outer * 2 + c, f)
        )

    def fan_copy(outer, core):
        slot = outer * 2 + core
        return remote(every.at[slot], every.at[slot], fan_send.at[outer], fan_recv.at[outer], partner)

    for i in range(1, no):
        cross_copy(along_outer(i), d).start()
    fan_copy(o, c).start()
    for i in range(1, no):
        outer = along_outer(i)
        cross_copy(outer, outer * 2 + c).wait_recv()
        fan_copy(outer, c).start()
    for i in range(no):
        fan_copy(along_outer(i), 1 - c).wait_recv()
    act_out[...] = every[...].reshape(act_out.shape)

    square.wait_side()
    for side in range(2):
        grad_out[:, pl.ds(side * width, width)] = sq_held[side].reshape(rows, width)

    grad.wait_sends()
    act.wait_sends()
    square.wait_sends()
    wait_sums(0)
    wait_sums(1)
    for i in range(1, no):
        cross_copy(along_outer(i), d).wait_send()
    for i in range(no):
        fan_copy(along_outer(i), c).wait_send()


def on_device(nd, nf, activations, gradients, act_basis, grad_basis):
    na, no = nf // 2, nd // 2
    tokens, width = activations.shape
    depth = act_basis.shape[0]
    bf16, f32 = jnp.bfloat16, jnp.float32
    dma = pltpu.SemaphoreType.DMA
    act_every, grad_block = pl.pallas_call(
        functools.partial(kernel, nd, na),
        out_shape=(
            jax.ShapeDtypeStruct((nd * tokens, width), bf16),
            jax.ShapeDtypeStruct((nd * tokens, 2 * width), bf16),
        ),
        in_specs=[pl.BlockSpec(memory_space=pl.ANY)] * 4,
        out_specs=[pl.BlockSpec(memory_space=pltpu.VMEM)] * 2,
        scratch_shapes=[
            pltpu.VMEM((2, depth, width), bf16),
            pltpu.VMEM((2, na, tokens, width), bf16),
            pltpu.VMEM((2, 2, nd, tokens, width), bf16),
            pltpu.VMEM((2, nd, tokens, width), f32),
            pltpu.VMEM((2, no, tokens, width), f32),
            pltpu.VMEM((2, no, tokens, width), f32),
            pltpu.VMEM((na, tokens, width), bf16),
            pltpu.VMEM((2, nd, tokens, width), bf16),
            pltpu.VMEM((nd, tokens, width), bf16),
            dma((4,)),
            dma((3, na)), dma((3, na)),
            dma((3, nd)), dma((3, nd)),
            dma((3, nd)), dma((3, nd)),
            dma((2, no)), dma((2, no)),
            dma((2, no)), dma((2, no)),
            dma((no,)), dma((no,)),
            dma((no,)), dma((no,)),
        ],
        compiler_params=pltpu.CompilerParams(
            collective_id=0, has_side_effects=True, vmem_limit_bytes=48 * 2**20
        ),
        cost_estimate=pl.CostEstimate(
            flops=4 * nd * tokens * depth * width,
            bytes_accessed=4 * depth * width + 10 * nd * tokens * width,
            transcendentals=0,
        ),
    )(gradients, activations, grad_basis, act_basis)
    total = lax.dot_general(
        act_every, grad_block, (((0,), (0,)), ((), ())), preferred_element_type=jnp.float32
    )
    return total * (1.0 / act_every.shape[0])


def solution(mesh):
    return jax.shard_map(
        functools.partial(on_device, mesh.shape["dp"], mesh.shape["factor"]),
        mesh=mesh,
        in_specs=(P("dp", "factor"), P("dp", "factor"), P("dp", "factor"), P("dp", "factor")),
        out_specs=P("factor", "dp"),
        check_vma=False,
    )
```

time: 292 us -> 135 us (0.46)
  the two profiles are of different devices: /device:TPU:29 before, /device:TPU:13 now
where the time goes in v2:
time: 135 us
  Pallas kernels  128 us (95%)
  matrix products  5.78 us (4%)
  local copies, waits for them, and re-layouts  1.9 us (1%)
    pallas_call x1, Pallas kernels, on_device(): pl.pallas_call(functools.partial(kernel, nd, na), out_shape=(jax.ShapeDty...  128 us
    dot_general x1, matrix products, on_device(): lax.dot_general(act_every, grad_block, (((0,), (0,)), ((), ())), preferre...  5.78 us

profile of v2, /device:TPU:13, one launch (start us, length us, event | category | flops | bytes accessed | tf_op | source)
XLA Modules:
  0.0 135.3 jit_solution(10905820017423794096)
XLA Ops:
  0.0 0.0 copy-start
  0.0 0.9 copy-done
  1.0 0.0 copy-start.1
  1.0 0.9 copy-done.1
  1.9 127.6 %shard_map.46 = (bf16[512,1024]{1,0:T(8,128)(2,1)S(1)}, bf16[512,2048]{1,0:T(8,128)(2,1)S(1)}) custom-call(bf16[128,1024]{1,0:T(8,128)(2,1)S(1)} %copy-done, bf16[128,1024]{1,0:T(8,128)(2,1)S(1)} %copy-done.1, bf16[2048,1024]{1,0:T(8,128)(2,1)} %grad_basis_hbm.1, bf16[2048,1024]{1,0:T(8,128)(2,1)} %act_basis_hbm.1), custom_call_target="tpu_custom_call" | custom-call | flops 4294967296 | bytes 13631488 | tf_op jit(solution)/shard_map/pallas_call | solution.py:257
  129.5 5.8 %convolution_multiply_fusion = f32[1024,2048]{1,0:T(8,128)} fusion(bf16[512,1024]{1,0:T(8,128)(2,1)S(1)} %get-tuple-element.7, bf16[512,2048]{1,0:T(8,128)(2,1)S(1)} %get-tuple-element.8), kind=kOutput, calls=%fused_computation | convolution fusion | flops 2149580800 | bytes 11534336 | tf_op jit(solution)/shard_map/dot_general | solution.py:293
Async XLA Ops:
  0.0 0.9 copy-start
  1.0 0.9 copy-start.1

commit v3 on v2

--- a/solution.py
+++ b/solution.py
@@ -42,11 +42,14 @@
     across = (d, a * 2 + 1 - b)
     partner = (o * 2 + 1 - c, f)
 
+    half = line.shape[2]
     loads = [
-        pltpu.make_async_copy(grad_hbm, line.at[0, a], load_sem.at[0]),
-        pltpu.make_async_copy(act_hbm, line.at[1, a], load_sem.at[1]),
-        pltpu.make_async_copy(grad_basis_hbm, basis.at[0], load_sem.at[2]),
-        pltpu.make_async_copy(act_basis_hbm, basis.at[1], load_sem.at[3]),
+        pltpu.make_async_copy(hbm.at[pl.ds(h * half, half)], line.at[2 * n + h, a], load_sem.at[2 * n + h])
+        for n, hbm in enumerate((grad_hbm, act_hbm))
+        for h in range(2)
+    ] + [
+        pltpu.make_async_copy(grad_basis_hbm, basis.at[0], load_sem.at[4]),
+        pltpu.make_async_copy(act_basis_hbm, basis.at[1], load_sem.at[5]),
     ]
     for load in loads:
         load.start()
@@ -90,7 +93,7 @@
 
         def forward_dp(self, steps):
             for i in steps:
-                panel = along_line(i)
+                panel = along_line(na - i)
                 if i:
                     self.line_copy(i, panel).wait_recv()
 
@@ -134,10 +137,10 @@
             columns = pl.ds(pl.multiple_of(tile * TILE, TILE), TILE)
             depth = held.shape[4]
             total = jnp.dot(
-                held[m, 0].reshape(rows, depth), basis[m, pl.ds(0, depth), columns],
+                held[m, 0].reshape(rows, depth), basis[m // 2, pl.ds(0, depth), columns],
                 preferred_element_type=jnp.float32,
             ) + jnp.dot(
-                held[m, 1].reshape(rows, depth), basis[m, pl.ds(depth, depth), columns],
+                held[m, 1].reshape(rows, depth), basis[m // 2, pl.ds(depth, depth), columns],
                 preferred_element_type=jnp.float32,
             )
             part[m, :, :, columns] = total.reshape(nd, rows // nd, TILE)
@@ -180,78 +183,107 @@
             if i < no:
                 tail_copy(m, along_outer(i), o).wait_send()
 
-    grad = Redistribute(0, line.at[0], held.at[0])
-    act = Redistribute(1, line.at[1], held.at[1])
-    square = Redistribute(2, sq_line, sq_held)
-
-    loads[0].wait()
-    grad.start_line()
-    loads[1].wait()
-    act.start_line()
-    grad.forward_dp(range(na))
-    act.forward_dp(range(1))
-    grad.forward_side(range(1, nd))
-    act.forward_dp(range(1, na - 1))
-    loads[2].wait()
-    grad.wait_side()
-    multiply(0)
-    start_pair(0)
-    act.forward_dp(range(na - 1, na))
+    moves = [Redistribute(m, line.at[m], held.at[m]) for m in range(4)]
+    squares = [Redistribute(4 + h, sq_line.at[h], sq_held.at[h]) for h in range(2)]
+
+    def start_line(m):
+        loads[m].wait()
+        moves[m].start_line()
+
+    def forward_dp(move):
+        move.forward_dp(range(na))
+
+    def forward_side(move):
+        move.forward_side(range(1, nd))
+
+    def rotate(m):
+        moves[m].wait_side()
+        multiply(m)
+        start_pair(m)
+
+    def spread_grad(h):
+        sq_line[h, a] = squared(h)
+        squares[h].start_line()
+
+    def cross_copy(h, outer, slot):
+        return remote(
+            every.at[h, d], every.at[h, slot], sq_send.at[h, outer], sq_recv.at[h, slot // 2],
+            (outer * 2 + c, f),
+        )
+
+    def fan_copy(h, outer, core):
+        slot = every.at[h, outer * 2 + core]
+        return remote(slot, slot, fan_send.at[h, outer], fan_recv.at[h, outer], partner)
+
+    def spread_act(h):
+        every[h, d] = squared(2 + h)
+        for i in range(1, no):
+            cross_copy(h, along_outer(i), d).start()
+        fan_copy(h, o, c).start()
+
+    def fan_act(h):
+        for i in range(1, no):
+            outer = along_outer(i)
+            cross_copy(h, outer, outer * 2 + c).wait_recv()
+            fan_copy(h, outer, c).start()
+
+    start_line(0)
+    start_line(1)
+    forward_dp(moves[0])
+    start_line(2)
+    forward_side(moves[0])
+    forward_dp(moves[1])
+    start_line(3)
+    forward_side(moves[1])
+    loads[4].wait()
+    rotate(0)
+    forward_dp(moves[2])
     start_tail(0)
-    act.forward_side(range(1, nd))
-    loads[3].wait()
-
-    sq_line[a] = squared(0)
-    square.start_line()
-    square.forward_dp(range(1))
-    act.wait_side()
-    multiply(1)
-    start_pair(1)
+    forward_side(moves[2])
+    rotate(1)
+    forward_dp(moves[3])
     start_tail(1)
-    square.forward_dp(range(1, na))
-    square.forward_side(range(1, nd))
-
-    every[d] = squared(1)
-
-    def cross_copy(outer, slot):
-        return remote(
-            every.at[d], every.at[slot], sq_send.at[outer], sq_recv.at[slot // 2], (outer * 2 + c, f)
-        )
-
-    def fan_copy(outer, core):
-        slot = outer * 2 + core
-        return remote(every.at[slot], every.at[slot], fan_send.at[outer], fan_recv.at[outer], partner)
-
-    for i in range(1, no):
-        cross_copy(along_outer(i), d).start()
-    fan_copy(o, c).start()
-    for i in range(1, no):
-        outer = along_outer(i)
-        cross_copy(outer, outer * 2 + c).wait_recv()
-        fan_copy(outer, c).start()
-    for i in range(no):
-        fan_copy(along_outer(i), 1 - c).wait_recv()
-    act_out[...] = every[...].reshape(act_out.shape)
-
-    square.wait_side()
-    for side in range(2):
-        grad_out[:, pl.ds(side * width, width)] = sq_held[side].reshape(rows, width)
-
-    grad.wait_sends()
-    act.wait_sends()
-    square.wait_sends()
-    wait_sums(0)
-    wait_sums(1)
-    for i in range(1, no):
-        cross_copy(along_outer(i), d).wait_send()
-    for i in range(no):
-        fan_copy(along_outer(i), c).wait_send()
+    spread_grad(0)
+    forward_side(moves[3])
+    loads[5].wait()
+    rotate(2)
+    forward_dp(squares[0])
+    start_tail(2)
+    spread_grad(1)
+    forward_side(squares[0])
+    rotate(3)
+    forward_dp(squares[1])
+    start_tail(3)
+    spread_act(0)
+    forward_side(squares[1])
+    spread_act(1)
+    fan_act(0)
+    fan_act(1)
+
+    for h in range(2):
+        squares[h].wait_side()
+        for side in range(2):
+            grad_out[pl.ds(h * rows, rows), pl.ds(side * width, width)] = sq_held[h, side].reshape(rows, width)
+    for h in range(2):
+        for i in range(no):
+            fan_copy(h, along_outer(i), 1 - c).wait_recv()
+        act_out[pl.ds(h * rows, rows), :] = every[h].reshape(rows, width)
+
+    for move in moves + squares:
+        move.wait_sends()
+    for m in range(4):
+        wait_sums(m)
+    for h in range(2):
+        for i in range(1, no):
+            cross_copy(h, along_outer(i), d).wait_send()
+        for i in range(no):
+            fan_copy(h, along_outer(i), c).wait_send()
 
 
 def on_device(nd, nf, activations, gradients, act_basis, grad_basis):
     na, no = nf // 2, nd // 2
     tokens, width = activations.shape
-    depth = act_basis.shape[0]
+    depth, half = act_basis.shape[0], tokens // 2
     bf16, f32 = jnp.bfloat16, jnp.float32
     dma = pltpu.SemaphoreType.DMA
     act_every, grad_block = pl.pallas_call(
@@ -264,22 +296,22 @@
         out_specs=[pl.BlockSpec(memory_space=pltpu.VMEM)] * 2,
         scratch_shapes=[
             pltpu.VMEM((2, depth, width), bf16),
-            pltpu.VMEM((2, na, tokens, width), bf16),
-            pltpu.VMEM((2, 2, nd, tokens, width), bf16),
-            pltpu.VMEM((2, nd, tokens, width), f32),
-            pltpu.VMEM((2, no, tokens, width), f32),
-            pltpu.VMEM((2, no, tokens, width), f32),
-            pltpu.VMEM((na, tokens, width), bf16),
-            pltpu.VMEM((2, nd, tokens, width), bf16),
-            pltpu.VMEM((nd, tokens, width), bf16),
-            dma((4,)),
-            dma((3, na)), dma((3, na)),
-            dma((3, nd)), dma((3, nd)),
-            dma((3, nd)), dma((3, nd)),
+            pltpu.VMEM((4, na, half, width), bf16),
+            pltpu.VMEM((4, 2, nd, half, width), bf16),
+            pltpu.VMEM((4, nd, half, width), f32),
+            pltpu.VMEM((4, no, half, width), f32),
+            pltpu.VMEM((4, no, half, width), f32),
+            pltpu.VMEM((2, na, half, width), bf16),
+            pltpu.VMEM((2, 2, nd, half, width), bf16),
+            pltpu.VMEM((2, nd, half, width), bf16),
+            dma((6,)),
+            dma((6, na)), dma((6, na)),
+            dma((6, nd)), dma((6, nd)),
+            dma((6, nd)), dma((6, nd)),
+            dma((4, no)), dma((4, no)),
+            dma((4, no)), dma((4, no)),
             dma((2, no)), dma((2, no)),
             dma((2, no)), dma((2, no)),
-            dma((no,)), dma((no,)),
-            dma((no,)), dma((no,)),
         ],
         compiler_params=pltpu.CompilerParams(
             collective_id=0, has_side_effects=True, vmem_limit_bytes=48 * 2**20

time: 135 us -> 109 us (0.81)
  the two profiles are of different devices: /device:TPU:13 before, /device:TPU:29 now
where the time goes in v3:
time: 109 us; the launch traced here: 108 us
  Pallas kernels  101 us (93%)
  matrix products  5.78 us (5%)
  local copies, waits for them, and re-layouts  1.9 us (2%)
    pallas_call x1, Pallas kernels, on_device(): pl.pallas_call(functools.partial(kernel, nd, na), out_shape=(jax.ShapeDty...  101 us
    dot_general x1, matrix products, on_device(): lax.dot_general(act_every, grad_block, (((0,), (0,)), ((), ())), preferre...  5.78 us

profile of v3, /device:TPU:29, one launch (start us, length us, event | category | flops | bytes accessed | tf_op | source)
XLA Modules:
  0.0 108.4 jit_solution(9849151266932311662)
XLA Ops:
  0.0 0.0 copy-start
  0.0 0.9 copy-done
  1.0 0.0 copy-start.1
  1.0 0.9 copy-done.1
  1.9 100.7 %shard_map.46 = (bf16[512,1024]{1,0:T(8,128)(2,1)S(1)}, bf16[512,2048]{1,0:T(8,128)(2,1)S(1)}) custom-call(bf16[128,1024]{1,0:T(8,128)(2,1)S(1)} %copy-done, bf16[128,1024]{1,0:T(8,128)(2,1)S(1)} %copy-done.1, bf16[2048,1024]{1,0:T(8,128)(2,1)} %grad_basis_hbm.1, bf16[2048,1024]{1,0:T(8,128)(2,1)} %act_basis_hbm.1), custom_call_target="tpu_custom_call" | custom-call | flops 4294967296 | bytes 13631488 | tf_op jit(solution)/shard_map/pallas_call | solution.py:289
  102.6 5.8 %convolution_multiply_fusion = f32[1024,2048]{1,0:T(8,128)} fusion(bf16[512,1024]{1,0:T(8,128)(2,1)S(1)} %get-tuple-element.7, bf16[512,2048]{1,0:T(8,128)(2,1)S(1)} %get-tuple-element.8), kind=kOutput, calls=%fused_computation | convolution fusion | flops 2149580800 | bytes 11534336 | tf_op jit(solution)/shard_map/dot_general | solution.py:325
Async XLA Ops:
  0.0 0.9 copy-start
  1.0 0.9 copy-start.1

commit v4 on v3

--- a/solution.py
+++ b/solution.py
@@ -39,6 +39,7 @@
             device_id=device, device_id_type=MESH,
         )
 
+    has_next = (a > 0, a + 1 < na)
     across = (d, a * 2 + 1 - b)
     partner = (o * 2 + 1 - c, f)
 
@@ -66,12 +67,18 @@
         def __init__(self, m, lines, blocks):
             self.m, self.lines, self.blocks = m, lines, blocks
 
-        def line_copy(self, i, slot):
-            m = self.m
+        def line_copy(self, slot, way):
+            m, step = self.m, 2 * way - 1
             return remote(
-                self.lines.at[a], self.lines.at[slot], z_send.at[m, i], z_recv.at[m, slot],
-                (d, along_line(i) * 2 + b),
+                self.lines.at[slot], self.lines.at[slot], z_send.at[m, way, slot], z_recv.at[m, slot],
+                (d, (a + step) * 2 + b),
             )
+
+        def line_arrived(self, slot):
+            remote(
+                self.lines.at[slot], self.lines.at[slot], z_send.at[self.m, 0, slot],
+                z_recv.at[self.m, slot], across,
+            ).wait_recv()
 
         def dp_copy(self, panel, slot):
             m = self.m
@@ -88,23 +95,35 @@
             )
 
         def start_line(self):
+            for way in range(2):
+                @pl.when(has_next[way])
+                def _():
+                    self.line_copy(a, way).start()
+
+        def start_dp(self, panel):
+            @pl.when(panel != d)
+            def _():
+                self.dp_copy(panel, d).start()
+
+            @pl.when(panel == d)
+            def _():
+                self.blocks[b, d] = self.lines[panel]
+                self.side_copy(b, d).start()
+
+        def forward_line(self):
             for i in range(1, na):
-                self.line_copy(i, a).start()
-
-        def forward_dp(self, steps):
-            for i in steps:
-                panel = along_line(na - i)
-                if i:
-                    self.line_copy(i, panel).wait_recv()
-
-                @pl.when(panel != d)
-                def _():
-                    self.dp_copy(panel, d).start()
-
-                @pl.when(panel == d)
-                def _():
-                    self.blocks[b, d] = self.lines[panel]
-                    self.side_copy(b, d).start()
+                for way in range(2):
+                    slot = a - i if way else a + i
+
+                    @pl.when(slot >= 0 if way else slot < na)
+                    def _():
+                        self.line_arrived(slot)
+
+                        @pl.when(has_next[way])
+                        def _():
+                            self.line_copy(slot, way).start()
+
+                        self.start_dp(slot)
 
         def forward_side(self, steps):
             for i in steps:
@@ -117,8 +136,13 @@
                 self.side_copy(1 - b, along_dp(i)).wait_recv()
 
         def wait_sends(self):
-            for i in range(1, na):
-                self.line_copy(i, a).wait_send()
+            for way in range(2):
+                for i in range(na):
+                    slot = a - i if way else a + i
+
+                    @pl.when(jnp.logical_and(slot >= 0 if way else slot < na, has_next[way]))
+                    def _():
+                        self.line_copy(slot, way).wait_send()
             for i in range(na):
                 panel = along_line(i)
 
@@ -189,9 +213,10 @@
     def start_line(m):
         loads[m].wait()
         moves[m].start_line()
+        moves[m].start_dp(a)
 
     def forward_dp(move):
-        move.forward_dp(range(na))
+        move.forward_line()
 
     def forward_side(move):
         move.forward_side(range(1, nd))
@@ -204,6 +229,7 @@
     def spread_grad(h):
         sq_line[h, a] = squared(h)
         squares[h].start_line()
+        squares[h].start_dp(a)
 
     def cross_copy(h, outer, slot):
         return remote(
@@ -305,7 +331,7 @@
             pltpu.VMEM((2, 2, nd, half, width), bf16),
             pltpu.VMEM((2, nd, half, width), bf16),
             dma((6,)),
-            dma((6, na)), dma((6, na)),
+            dma((6, 2, na)), dma((6, na)),
             dma((6, nd)), dma((6, nd)),
             dma((6, nd)), dma((6, nd)),
             dma((4, no)), dma((4, no)),

time: 109 us -> 99.8 us (0.916)
  Pallas kernels: 101 us -> 91.7 us
    pallas_call x1, Pallas kernels: 101 us -> 91.7 us  [on_device(): pl.pallas_call(functools.partial(kernel, nd, na), out_shape=(jax.ShapeDty...]
where the time goes in v4:
time: 99.8 us; the launch traced here: 99.4 us
  Pallas kernels  91.7 us (92%)
  matrix products  5.78 us (6%)
  local copies, waits for them, and re-layouts  1.9 us (2%)
    pallas_call x1, Pallas kernels, on_device(): pl.pallas_call(functools.partial(kernel, nd, na), out_shape=(jax.ShapeDty...  91.7 us
    dot_general x1, matrix products, on_device(): lax.dot_general(act_every, grad_block, (((0,), (0,)), ((), ())), preferre...  5.78 us

profile of v4, /device:TPU:29, one launch (start us, length us, event | category | flops | bytes accessed | tf_op | source)
XLA Modules:
  0.0 99.4 jit_solution(719195734809665621)
XLA Ops:
  0.0 0.0 copy-start
  0.0 0.9 copy-done
  1.0 0.0 copy-start.1
  1.0 0.9 copy-done.1
  1.9 91.7 %shard_map.46 = (bf16[512,1024]{1,0:T(8,128)(2,1)S(1)}, bf16[512,2048]{1,0:T(8,128)(2,1)S(1)}) custom-call(bf16[128,1024]{1,0:T(8,128)(2,1)S(1)} %copy-done, bf16[128,1024]{1,0:T(8,128)(2,1)S(1)} %copy-done.1, bf16[2048,1024]{1,0:T(8,128)(2,1)} %grad_basis_hbm.1, bf16[2048,1024]{1,0:T(8,128)(2,1)} %act_basis_hbm.1), custom_call_target="tpu_custom_call" | custom-call | flops 4294967296 | bytes 13631488 | tf_op jit(solution)/shard_map/pallas_call | solution.py:315
  93.6 5.8 %convolution_multiply_fusion = f32[1024,2048]{1,0:T(8,128)} fusion(bf16[512,1024]{1,0:T(8,128)(2,1)S(1)} %get-tuple-element.7, bf16[512,2048]{1,0:T(8,128)(2,1)S(1)} %get-tuple-element.8), kind=kOutput, calls=%fused_computation | convolution fusion | flops 2149580800 | bytes 11534336 | tf_op jit(solution)/shard_map/dot_general | solution.py:351
Async XLA Ops:
  0.0 0.9 copy-start
  1.0 0.9 copy-start.1

commit v5 on v4

--- a/solution.py
+++ b/solution.py
@@ -15,7 +15,7 @@
     nd, na,
     grad_hbm, act_hbm, grad_basis_hbm, act_basis_hbm,
     act_out, grad_out,
-    basis, line, held, part, pair, tail, sq_line, sq_held, every,
+    basis, line, wide, held, part, pair, tail, sq_line, sq_held, every,
     load_sem, z_send, z_recv, y_send, y_recv, x_send, x_recv,
     pair_send, pair_recv, tail_send, tail_recv, sq_send, sq_recv, fan_send, fan_recv,
 ):
@@ -45,7 +45,11 @@
 
     half = line.shape[2]
     loads = [
-        pltpu.make_async_copy(hbm.at[pl.ds(h * half, half)], line.at[2 * n + h, a], load_sem.at[2 * n + h])
+        pltpu.make_async_copy(
+            hbm.at[pl.ds(h * half, half)],
+            wide.at[b, a] if n and h else line.at[2 * n + h, a],
+            load_sem.at[2 * n + h],
+        )
         for n, hbm in enumerate((grad_hbm, act_hbm))
         for h in range(2)
     ] + [
@@ -64,8 +68,8 @@
     pl.semaphore_wait(barrier, na + nd - 1)
 
     class Redistribute:
-        def __init__(self, m, lines, blocks):
-            self.m, self.lines, self.blocks = m, lines, blocks
+        def __init__(self, m, lines, blocks, side, crosses=True):
+            self.m, self.lines, self.blocks, self.side, self.crosses = m, lines, blocks, side, crosses
 
         def line_copy(self, slot, way):
             m, step = self.m, 2 * way - 1
@@ -83,7 +87,7 @@
         def dp_copy(self, panel, slot):
             m = self.m
             return remote(
-                self.lines.at[panel], self.blocks.at[b, slot], y_send.at[m, panel], y_recv.at[m, slot],
+                self.lines.at[panel], self.blocks.at[self.side, slot], y_send.at[m, panel], y_recv.at[m, slot],
                 (panel, f),
             )
 
@@ -107,8 +111,9 @@
 
             @pl.when(panel == d)
             def _():
-                self.blocks[b, d] = self.lines[panel]
-                self.side_copy(b, d).start()
+                self.blocks[self.side, d] = self.lines[panel]
+                if self.crosses:
+                    self.side_copy(b, d).start()
 
         def forward_line(self):
             for i in range(1, na):
@@ -129,7 +134,8 @@
             for i in steps:
                 rows = along_dp(i)
                 self.dp_copy(d, rows).wait_recv()
-                self.side_copy(b, rows).start()
+                if self.crosses:
+                    self.side_copy(b, rows).start()
 
         def wait_side(self):
             for i in range(nd):
@@ -149,7 +155,7 @@
                 @pl.when(panel != d)
                 def _():
                     self.dp_copy(panel, d).wait_send()
-            for i in range(nd):
+            for i in range(nd if self.crosses else 0):
                 self.side_copy(b, along_dp(i)).wait_send()
 
     width = part.shape[-1]
@@ -207,8 +213,15 @@
             if i < no:
                 tail_copy(m, along_outer(i), o).wait_send()
 
-    moves = [Redistribute(m, line.at[m], held.at[m]) for m in range(4)]
-    squares = [Redistribute(4 + h, sq_line.at[h], sq_held.at[h]) for h in range(2)]
+    moves = [Redistribute(m, line.at[m], held.at[m], b) for m in range(3)]
+    squares = [Redistribute(4 + h, sq_line.at[h], sq_held.at[h], b) for h in range(2)]
+    both = [
+        Redistribute(3, wide.at[b], held.at[3], b, False),
+        Redistribute(6, wide.at[1 - b], held.at[3], 1 - b, False),
+    ]
+
+    def first_copy(side):
+        return remote(wide.at[side, a], wide.at[side, a], x_send.at[3, 0], x_recv.at[3, 0], across)
 
     def start_line(m):
         loads[m].wait()
@@ -222,7 +235,11 @@
         move.forward_side(range(1, nd))
 
     def rotate(m):
-        moves[m].wait_side()
+        if m < 3:
+            moves[m].wait_side()
+        else:
+            for move in both:
+                forward_side(move)
         multiply(m)
         start_pair(m)
 
@@ -255,11 +272,16 @@
 
     start_line(0)
     start_line(1)
+    loads[3].wait()
+    first_copy(b).start()
     forward_dp(moves[0])
     start_line(2)
     forward_side(moves[0])
     forward_dp(moves[1])
-    start_line(3)
+    first_copy(1 - b).wait_recv()
+    for move in both:
+        move.start_line()
+        move.start_dp(a)
     forward_side(moves[1])
     loads[4].wait()
     rotate(0)
@@ -267,10 +289,10 @@
     start_tail(0)
     forward_side(moves[2])
     rotate(1)
-    forward_dp(moves[3])
+    for move in both:
+        forward_dp(move)
     start_tail(1)
     spread_grad(0)
-    forward_side(moves[3])
     loads[5].wait()
     rotate(2)
     forward_dp(squares[0])
@@ -295,8 +317,9 @@
             fan_copy(h, along_outer(i), 1 - c).wait_recv()
         act_out[pl.ds(h * rows, rows), :] = every[h].reshape(rows, width)
 
-    for move in moves + squares:
+    for move in moves + both + squares:
         move.wait_sends()
+    first_copy(b).wait_send()
     for m in range(4):
         wait_sums(m)
     for h in range(2):
@@ -322,7 +345,8 @@
         out_specs=[pl.BlockSpec(memory_space=pltpu.VMEM)] * 2,
         scratch_shapes=[
             pltpu.VMEM((2, depth, width), bf16),
-            pltpu.VMEM((4, na, half, width), bf16),
+            pltpu.VMEM((3, na, half, width), bf16),
+            pltpu.VMEM((2, na, half, width), bf16),
             pltpu.VMEM((4, 2, nd, half, width), bf16),
             pltpu.VMEM((4, nd, half, width), f32),
             pltpu.VMEM((4, no, half, width), f32),
@@ -331,8 +355,8 @@
             pltpu.VMEM((2, 2, nd, half, width), bf16),
             pltpu.VMEM((2, nd, half, width), bf16),
             dma((6,)),
-            dma((6, 2, na)), dma((6, na)),
-            dma((6, nd)), dma((6, nd)),
+            dma((7, 2, na)), dma((7, na)),
+            dma((7, nd)), dma((7, nd)),
             dma((6, nd)), dma((6, nd)),
             dma((4, no)), dma((4, no)),
             dma((4, no)), dma((4, no)),

time: 99.8 us -> 105 us (1.052)
  the two profiles are of different devices: /device:TPU:29 before, /device:TPU:1 now
where the time goes in v5:
time: 105 us
  Pallas kernels  97.3 us (93%)
  matrix products  5.78 us (6%)
  local copies, waits for them, and re-layouts  1.9 us (2%)
    pallas_call x1, Pallas kernels, on_device(): pl.pallas_call(functools.partial(kernel, nd, na), out_shape=(jax.ShapeDty...  97.3 us
    dot_general x1, matrix products, on_device(): lax.dot_general(act_every, grad_block, (((0,), (0,)), ((), ())), preferre...  5.78 us

profile of v5, /device:TPU:1, one launch (start us, length us, event | category | flops | bytes accessed | tf_op | source)
XLA Modules:
  0.0 105.0 jit_solution(15215653171381204284)
XLA Ops:
  0.0 0.0 copy-start
  0.0 0.9 copy-done
  1.0 0.0 copy-start.1
  1.0 0.9 copy-done.1
  1.9 97.3 %shard_map.46 = (bf16[512,1024]{1,0:T(8,128)(2,1)S(1)}, bf16[512,2048]{1,0:T(8,128)(2,1)S(1)}) custom-call(bf16[128,1024]{1,0:T(8,128)(2,1)S(1)} %copy-done, bf16[128,1024]{1,0:T(8,128)(2,1)S(1)} %copy-done.1, bf16[2048,1024]{1,0:T(8,128)(2,1)} %grad_basis_hbm.1, bf16[2048,1024]{1,0:T(8,128)(2,1)} %act_basis_hbm.1), custom_call_target="tpu_custom_call" | custom-call | flops 4294967296 | bytes 13631488 | tf_op jit(solution)/shard_map/pallas_call | solution.py:338
  99.2 5.8 %convolution_multiply_fusion = f32[1024,2048]{1,0:T(8,128)} fusion(bf16[512,1024]{1,0:T(8,128)(2,1)S(1)} %get-tuple-element.7, bf16[512,2048]{1,0:T(8,128)(2,1)S(1)} %get-tuple-element.8), kind=kOutput, calls=%fused_computation | convolution fusion | flops 2149580800 | bytes 11534336 | tf_op jit(solution)/shard_map/dot_general | solution.py:375
Async XLA Ops:
  0.0 0.9 copy-start
  1.0 0.9 copy-start.1

commit v6 on v4

--- a/solution.py
+++ b/solution.py
@@ -261,13 +261,13 @@
     forward_dp(moves[1])
     start_line(3)
     forward_side(moves[1])
+    forward_dp(moves[2])
     loads[4].wait()
     rotate(0)
-    forward_dp(moves[2])
     start_tail(0)
     forward_side(moves[2])
+    forward_dp(moves[3])
     rotate(1)
-    forward_dp(moves[3])
     start_tail(1)
     spread_grad(0)
     forward_side(moves[3])
@@ -282,8 +282,8 @@
     start_tail(3)
     spread_act(0)
     forward_side(squares[1])
+    fan_act(0)
     spread_act(1)
-    fan_act(0)
     fan_act(1)
 
     for h in range(2):

time: 99.8 us -> 102 us (1.022)
  Pallas kernels: 91.7 us -> 94.5 us
    pallas_call x1, Pallas kernels: 91.7 us -> 94.5 us  [on_device(): pl.pallas_call(functools.partial(kernel, nd, na), out_shape=(jax.ShapeDty...]
where the time goes in v6:
time: 102 us
  Pallas kernels  94.5 us (93%)
  matrix products  5.78 us (6%)
  local copies, waits for them, and re-layouts  1.9 us (2%)
    pallas_call x1, Pallas kernels, on_device(): pl.pallas_call(functools.partial(kernel, nd, na), out_shape=(jax.ShapeDty...  94.5 us
    dot_general x1, matrix products, on_device(): lax.dot_general(act_every, grad_block, (((0,), (0,)), ((), ())), preferre...  5.78 us

profile of v6, /device:TPU:29, one launch (start us, length us, event | category | flops | bytes accessed | tf_op | source)
XLA Modules:
  0.0 102.2 jit_solution(7938339159007548441)
XLA Ops:
  0.0 0.0 copy-start
  0.0 0.9 copy-done
  1.0 0.0 copy-start.1
  1.0 0.9 copy-done.1
  1.9 94.5 %shard_map.46 = (bf16[512,1024]{1,0:T(8,128)(2,1)S(1)}, bf16[512,2048]{1,0:T(8,128)(2,1)S(1)}) custom-call(bf16[128,1024]{1,0:T(8,128)(2,1)S(1)} %copy-done, bf16[128,1024]{1,0:T(8,128)(2,1)S(1)} %copy-done.1, bf16[2048,1024]{1,0:T(8,128)(2,1)} %grad_basis_hbm.1, bf16[2048,1024]{1,0:T(8,128)(2,1)} %act_basis_hbm.1), custom_call_target="tpu_custom_call" | custom-call | flops 4294967296 | bytes 13631488 | tf_op jit(solution)/shard_map/pallas_call | solution.py:315
  96.4 5.8 %convolution_multiply_fusion = f32[1024,2048]{1,0:T(8,128)} fusion(bf16[512,1024]{1,0:T(8,128)(2,1)S(1)} %get-tuple-element.7, bf16[512,2048]{1,0:T(8,128)(2,1)S(1)} %get-tuple-element.8), kind=kOutput, calls=%fused_computation | convolution fusion | flops 2149580800 | bytes 11534336 | tf_op jit(solution)/shard_map/dot_general | solution.py:351
Async XLA Ops:
  0.0 0.9 copy-start
  1.0 0.9 copy-start.1
